TPU v7x, 32 devices: a whole 2x2x4 slice. The times are simulated.
32 devices in a mesh: dp: 32 (over z, y, x, core).
Axes of the slice: x: 2, y: 2, z: 4, core: 2. Of those that a mesh axis runs over, the one named last changes fastest.
Arguments:
- images: bfloat16 [320, 16, 16, 3], P('dp'), may hold values from -6 to 6
- labels: int32 [320], P('dp'), may hold values from 0 to 9
- groups: int32 [320], P('dp'), may hold values from 0 to 1
- conv_w: float32 [4608, 256], P('dp'), may hold values from -0.125 to 0.125
- conv_m: float32 [4608, 256], P('dp'), may hold values from -0.00061035156 to 0.00061035156
- conv_v: float32 [4608, 256], P('dp'), may hold values from 1.2207031e-09 to 4.8828124e-09
- rot_bases: float32 [4, 256, 256], replicated, as said below
- stem_w: float32 [27, 256], replicated, may hold values from -1.25 to 1.25
- stem_m: float32 [27, 256], replicated, may hold values from -0.00061035156 to 0.00061035156
- stem_v: float32 [27, 256], replicated, may hold values from 1.2207031e-09 to 4.8828124e-09
- head_w: float32 [257, 10], replicated, may hold values from -4 to 4
- head_m: float32 [257, 10], replicated, may hold values from -0.0390625 to 0.0390625
- head_v: float32 [257, 10], replicated, may hold values from 5e-06 to 2e-05
- norm_p: float32 [6, 256], replicated
- norm_m: float32 [6, 256], replicated, may hold values from -0.0012207031 to 0.0012207031
- norm_v: float32 [6, 256], replicated, may hold values from 2.1875e-05 to 8.75e-05
Outputs:
- loss: float32 [2], replicated
- factors: float32 [1024, 256], P('dp')
- inverses: float32 [1024, 256], P('dp')
- conv_w_new: float32 [4608, 256], P('dp')
- conv_m_new: float32 [4608, 256], P('dp')
- conv_v_new: float32 [4608, 256], P('dp')
- rot_bases_new: float32 [4, 256, 256], replicated
- stem_w_new: float32 [27, 256], replicated
- stem_m_new: float32 [27, 256], replicated
- stem_v_new: float32 [27, 256], replicated
- head_w_new: float32 [257, 10], replicated
- head_m_new: float32 [257, 10], replicated
- head_v_new: float32 [257, 10], replicated
- norm_p_new: float32 [6, 256], replicated
- norm_m_new: float32 [6, 256], replicated
- norm_v_new: float32 [6, 256], replicated
- conv_bf16: bfloat16 [4608, 256], P('dp')
Inputs may be any that keep to these rules, and one draw needn't show every extreme that they name: `rot_bases`: each of the four matrices is orthogonal.
All inputs are finite; a program needn't handle non-finite values.
Results may differ from a plain program's by a relative error of at most 0.012.
The roundings to bfloat16 on the way count: a program that leaves them out, or rounds other values in their place, can miss the bound.
Values may be sent and summed in bfloat16 or wider, within the bound.
No kernel may reach another device: no remote copies, remote signals or barrier semaphores. Data moves between devices by JAX's collectives and lax.ppermute only.
A program may use at most 192 MiB of HBM per device.

v0:
```python
import math

import jax
import jax.numpy as jnp
from jax import lax
from jax.sharding import PartitionSpec as P

CLASSES = 10
NS_ITERS = 6
STEP = 5


EPS_NORM = 1e-05
BETA_ONE = 0.9
BETA_TWO = 0.99
ADAM_EPS = 1e-08
WEIGHT_DECAY = 0.01
DAMPING = 0.1
PROBIT_SCALE = math.pi / 8.0
RATE_CONV = 0.02
RATE_STEM = 0.1
RATE_HEAD = 0.1
RATE_NORM = 0.5
highest = lax.Precision.HIGHEST


def to_blocks(rows_in, count):
    width = rows_in.shape[1]
    return rows_in.reshape(width, count, width).transpose(1, 0, 2)


def from_blocks(stacked):
    return stacked.transpose(1, 0, 2).reshape(-1, stacked.shape[2])


def patches(images_in):
    side_len = images_in.shape[1]
    padded = jnp.pad(images_in, ((0, 0), (1, 1), (1, 1), (0, 0)))
    pieces = [
        padded[:, offset_a : offset_a + side_len, offset_b : offset_b + side_len, :]
        for offset_a in range(3)
        for offset_b in range(3)
    ]
    return jnp.concatenate(pieces, axis=-1).reshape(-1, 9 * images_in.shape[-1])


def inner_rows(left_in, right_in):
    return lax.dot_general(
        left_in, right_in, (((0,), (0,)), ((), ())), preferred_element_type=jnp.float32
    )


def moments(values):
    return jnp.stack([jnp.sum(values, axis=0), jnp.sum(values * values, axis=0)])


def pool_stats(values, extra):
    return lax.psum((moments(values), extra), "dp")


def normalize(values, stat_sums, gain_row, shift_row, pixels):
    mean_val = stat_sums[0] / pixels
    variance = stat_sums[1] / pixels - mean_val * mean_val
    inv_std = lax.rsqrt(variance + EPS_NORM)
    centered = (values - mean_val) * inv_std
    return (centered * gain_row + shift_row, centered, inv_std)


def norm_back(grad_out, centered, inv_std, gain_row, pixels):
    local_sums = jnp.stack([jnp.sum(grad_out, axis=0), jnp.sum(grad_out * centered, axis=0)])
    total_sums = lax.psum(local_sums, "dp")
    grad_in = (
        inv_std
        * gain_row
        * (grad_out - total_sums[0] / pixels - centered * (total_sums[1] / pixels))
    )
    return (grad_in, total_sums)


def gelu_back(pre_act, grad_out):
    return jax.vjp(jax.nn.gelu, pre_act)[1](grad_out)[0]


def layer_forward(inputs, stat_sums, gain_row, shift_row, weight, pixels, count_img, side_len):
    pre_act, centered, inv_std = normalize(inputs, stat_sums, gain_row, shift_row, pixels)
    hidden = jax.nn.gelu(pre_act).astype(jnp.bfloat16)
    columns = patches(hidden.reshape(count_img, side_len, side_len, -1))
    output = jnp.dot(columns, weight, preferred_element_type=jnp.float32)
    return (output, (pre_act, centered, inv_std, hidden, columns))


def layer_backward(grad_out, kept_vals, gain_row, weight, pixels, count_img, side_len):
    pre_act, centered, inv_std, hidden, columns = kept_vals
    channels = weight.shape[1]
    grad_low = grad_out.astype(jnp.bfloat16)
    weight_grad = inner_rows(columns, grad_low)
    flipped = (
        weight.reshape(9, channels, channels)[::-1]
        .transpose(0, 2, 1)
        .reshape(9 * channels, channels)
    )
    grad_hidden = jnp.dot(
        patches(grad_low.reshape(count_img, side_len, side_len, channels)),
        flipped,
        preferred_element_type=jnp.float32,
    )
    grad_pre = gelu_back(pre_act, grad_hidden)
    grad_in, total_sums = norm_back(grad_pre, centered, inv_std, gain_row, pixels)
    factor_a = inner_rows(hidden, hidden) / pixels
    factor_g = inner_rows(grad_low, grad_low) * pixels
    return (grad_in, weight_grad, total_sums, factor_a, factor_g)


def adam_step(param_in, grad_in, first_in, second_in, rate_in, decay_in):
    first_new = BETA_ONE * first_in + (1.0 - BETA_ONE) * grad_in
    second_new = BETA_TWO * second_in + (1.0 - BETA_TWO) * grad_in * grad_in
    direction = (
        first_new
        / (1.0 - BETA_ONE**STEP)
        / (jnp.sqrt(second_new / (1.0 - BETA_TWO**STEP)) + ADAM_EPS)
    )
    return (param_in - rate_in * (direction + decay_in * param_in), first_new, second_new)


def select_rows(stacked, pick_mask):
    return jnp.sum(stacked * pick_mask[:, :, None], axis=1)


def rotate_rows(selector, stacked, block_ids, layer_ids, right_q, pattern):
    mixed_rows = jnp.einsum("rk,bkn->rbn", selector, stacked, precision=highest)
    pick_block = (
        block_ids[:, None] == jnp.arange(stacked.shape[0], dtype=jnp.int32)[None, :]
    ).astype(jnp.float32)
    left_rows = select_rows(mixed_rows, pick_block)
    both_sides = jnp.einsum(pattern, left_rows, right_q, precision=highest)
    pick_layer = (layer_ids[:, None] == jnp.arange(2, dtype=jnp.int32)[None, :]).astype(jnp.float32)
    return select_rows(both_sides, pick_layer)


def damp_all(factor_full, channels):
    identity = jnp.eye(channels, dtype=jnp.float32)
    traces = jnp.trace(factor_full, axis1=1, axis2=2)
    return factor_full + (DAMPING * traces / channels)[:, None, None] * identity


def local(
    images,
    labels,
    groups,
    conv_w,
    conv_m,
    conv_v,
    rot_bases,
    stem_w,
    stem_m,
    stem_v,
    head_w,
    head_m,
    head_v,
    norm_p,
    norm_m,
    norm_v,
):
    devices = lax.axis_size("dp")
    my_index = lax.axis_index("dp")
    count_img, side_len = (images.shape[0], images.shape[1])
    channels = conv_w.shape[1]
    pixels = count_img * side_len * side_len * devices
    conv_gathered = lax.all_gather(conv_w.astype(jnp.bfloat16), "dp", axis=0, tiled=True)
    conv_full = to_blocks(conv_gathered, 18).reshape(18 * channels, channels)
    weights_img = 1.0 + 3.0 * groups.astype(jnp.float32)
    stem_cols = patches(images)
    stem_out = jnp.dot(stem_cols, stem_w.astype(jnp.bfloat16), preferred_element_type=jnp.float32)
    stat_sums, weight_total = pool_stats(stem_out, jnp.sum(weights_img))
    current = stem_out
    kept_all = []
    for layer_id in range(2):
        if layer_id > 0:
            stat_sums = pool_stats(current, jnp.zeros((), jnp.float32))[0]
        weight = conv_full[layer_id * 9 * channels : (layer_id + 1) * 9 * channels]
        current, kept_vals = layer_forward(
            current,
            stat_sums,
            norm_p[2 * layer_id],
            norm_p[2 * layer_id + 1],
            weight,
            pixels,
            count_img,
            side_len,
        )
        kept_all.append(kept_vals)
    residual = stem_out + current
    stat_sums = pool_stats(residual, jnp.zeros((), jnp.float32))[0]
    pre_last, centered_last, inv_last = normalize(residual, stat_sums, norm_p[4], norm_p[5], pixels)
    features = jax.nn.gelu(pre_last)
    pooled = jnp.mean(features.reshape(count_img, side_len * side_len, channels), axis=1)
    pooled_low = pooled.astype(jnp.bfloat16)
    head_low = head_w[:channels].astype(jnp.bfloat16)
    logits = jnp.dot(pooled_low, head_low, preferred_element_type=jnp.float32) + head_w[channels]
    spread = jnp.mean(pooled * pooled, axis=1)
    shrink = lax.rsqrt(1.0 + PROBIT_SCALE * spread)
    scaled = logits * shrink[:, None]
    targets = (labels[:, None] == jnp.arange(CLASSES, dtype=jnp.int32)[None, :]).astype(jnp.float32)
    log_total = jax.nn.logsumexp(scaled, axis=1)
    loss_local = jnp.sum(weights_img * (log_total - jnp.sum(scaled * targets, axis=1)))
    grad_scaled = (jnp.exp(scaled - log_total[:, None]) - targets) * (weights_img / weight_total)[
        :, None
    ]
    grad_logits = (grad_scaled * shrink[:, None]).astype(jnp.bfloat16)
    grad_shrink = jnp.sum(grad_scaled * logits, axis=1)
    grad_spread = grad_shrink * (-0.5 * PROBIT_SCALE) * shrink * shrink * shrink
    grad_pooled = lax.dot_general(
        grad_logits, head_low, (((1,), (1,)), ((), ())), preferred_element_type=jnp.float32
    )
    grad_pooled = grad_pooled + grad_spread[:, None] * 2.0 * pooled / channels
    head_grad = jnp.concatenate(
        [
            inner_rows(pooled_low, grad_logits),
            jnp.sum(grad_logits.astype(jnp.float32), axis=0)[None, :],
        ],
        axis=0,
    )
    grad_feat = jnp.broadcast_to(
        grad_pooled[:, None, :] / (side_len * side_len), (count_img, side_len * side_len, channels)
    ).reshape(-1, channels)
    grad_res, sums_last = norm_back(
        gelu_back(pre_last, grad_feat), centered_last, inv_last, norm_p[4], pixels
    )
    current = grad_res
    conv_grads = [None, None]
    norm_sums = [None, None, sums_last]
    factor_list = [None, None, None, None]
    for layer_id in (1, 0):
        weight = conv_full[layer_id * 9 * channels : (layer_id + 1) * 9 * channels]
        current, weight_grad, total_sums, factor_a, factor_g = layer_backward(
            current, kept_all[layer_id], norm_p[2 * layer_id], weight, pixels, count_img, side_len
        )
        conv_grads[layer_id] = weight_grad
        norm_sums[layer_id] = total_sums
        factor_list[2 * layer_id] = factor_a
        factor_list[2 * layer_id + 1] = factor_g
    grad_stem_out = (current + grad_res).astype(jnp.bfloat16)
    stem_grad = inner_rows(stem_cols, grad_stem_out)
    norm_grad = jnp.stack(
        [
            norm_sums[0][1],
            norm_sums[0][0],
            norm_sums[1][1],
            norm_sums[1][0],
            norm_sums[2][1],
            norm_sums[2][0],
        ]
    )
    conv_grad = from_blocks(jnp.concatenate(conv_grads, axis=0).reshape(18, channels, channels))
    factor_stack = from_blocks(jnp.stack(factor_list))
    factor_count = factor_stack.shape[0] // devices
    identity = jnp.eye(channels, dtype=jnp.float32)
    factor_all = lax.psum(factor_stack, "dp")
    factor_full = to_blocks(factor_all, 4)
    damped = damp_all(factor_full, channels)
    inverse = identity / jnp.sqrt(jnp.sum(damped * damped, axis=(1, 2)))[:, None, None]
    for sweep_id in range(NS_ITERS):
        product = jnp.einsum("mab,mbc->mac", inverse, damped, precision=highest)
        inverse = 2.0 * inverse - jnp.einsum("mab,mbc->mac", product, inverse, precision=highest)
    row_factor = lax.dynamic_slice_in_dim(factor_all, my_index * factor_count, factor_count, 0)
    inverse_rows = lax.dynamic_slice_in_dim(
        from_blocks(inverse), my_index * factor_count, factor_count, 0
    )
    turned = jnp.einsum("mab,mbc->mac", damped, rot_bases, precision=highest)
    gram_mat = jnp.einsum("mba,mbc->mac", turned, turned, precision=highest)
    lower_f = jnp.linalg.cholesky(gram_mat)
    bases_new = lax.linalg.triangular_solve(
        lower_f, turned, left_side=False, lower=True, transpose_a=True
    )
    left_q = rot_bases[0::2]
    right_q = rot_bases[1::2]
    row_count = conv_w.shape[0]
    global_row = my_index * row_count + jnp.arange(row_count, dtype=jnp.int32)
    block_ids = global_row % 18
    inner_ids = global_row // 18
    layer_ids = block_ids // 9
    conv_total, stem_total, head_total, loss_total = lax.psum(
        (conv_grad, stem_grad, head_grad, loss_local), "dp"
    )
    selector = left_q.transpose(0, 2, 1)[layer_ids, inner_ids]
    rotated = rotate_rows(
        selector, to_blocks(conv_total, 18), block_ids, layer_ids, right_q, "rn,lnd->rld"
    )
    first_conv = BETA_ONE * conv_m + (1.0 - BETA_ONE) * rotated
    second_conv = BETA_TWO * conv_v + (1.0 - BETA_TWO) * rotated * rotated
    direction = (
        first_conv
        / (1.0 - BETA_ONE**STEP)
        / (jnp.sqrt(second_conv / (1.0 - BETA_TWO**STEP)) + ADAM_EPS)
    )
    steps_full = to_blocks(lax.all_gather(direction, "dp", axis=0, tiled=True), 18)
    update = rotate_rows(
        left_q[layer_ids, inner_ids], steps_full, block_ids, layer_ids, right_q, "rn,ldn->rld"
    )
    conv_new = conv_w - RATE_CONV * (update + WEIGHT_DECAY * conv_w)
    stem_new, stem_first, stem_second = adam_step(
        stem_w, stem_total, stem_m, stem_v, RATE_STEM, WEIGHT_DECAY
    )
    head_new, head_first, head_second = adam_step(
        head_w, head_total, head_m, head_v, RATE_HEAD, WEIGHT_DECAY
    )
    norm_new, norm_first, norm_second = adam_step(norm_p, norm_grad, norm_m, norm_v, RATE_NORM, 0.0)
    loss = jnp.stack([loss_total, weight_total])
    return (
        loss,
        row_factor,
        inverse_rows,
        conv_new,
        first_conv,
        second_conv,
        bases_new,
        stem_new,
        stem_first,
        stem_second,
        head_new,
        head_first,
        head_second,
        norm_new,
        norm_first,
        norm_second,
        conv_new.astype(jnp.bfloat16),
    )


def solution(mesh):
    return jax.shard_map(
        local,
        mesh=mesh,
        in_specs=(
            P("dp", None, None, None),
            P("dp"),
            P("dp"),
            P("dp", None),
            P("dp", None),
            P("dp", None),
            P(),
            P(),
            P(),
            P(),
            P(),
            P(),
            P(),
            P(),
            P(),
            P(),
        ),
        out_specs=(
            P(),
            P("dp", None),
            P("dp", None),
            P("dp", None),
            P("dp", None),
            P("dp", None),
            P(),
            P(),
            P(),
            P(),
            P(),
            P(),
            P(),
            P(),
            P(),
            P(),
            P("dp", None),
        ),
        check_vma=False,
    )
```

profile of v0, /device:TPU:0, one launch (start us, length us, event | category | flops | bytes accessed | tf_op | source)
XLA Modules:
  0.0 861.1 jit_solution(12706718044288938510)
XLA Ops:
  21.5 42.5 %psum.84 = f32[2,256]{1,0:T(2,128)S(1)} all-reduce(f32[2,256]{1,0:T(2,128)S(1)} %pad_maximum_fusion.3), channel_id=1, replica_groups=mesh['dp'=32] {'dp'}, use_global_device_ids=true, to_apply=%region_2.3 | all-reduce | flops 512 | bytes 4096 | tf_op jit(solution)/shard_map/psum | solution.py:58
  107.8 6.2 rev.6
  116.0 9.2 %fusion.113 = (f32[256]{0:T(256)S(1)}, f32[256]{0:T(256)S(1)}, f32[2560,256]{1,0:T(8,128)}) fusion(bf16[2560,2304]{1,0:T(8,128)(2,1)} %constant_dynamic-update-slice_fusion.1, bf16[2304,256]{1,0:T(8,128)(2,1)S(1)} %bitcast.287), kind=kOutput, calls=%fused_computation.332 | convolution fusion | flops 3021864448 | bytes 15599616 | tf_op jit(solution)/shard_map/dot_general | solution.py:88
  125.2 40.3 %psum.85 = f32[2,256]{1,0:T(2,128)S(1)} all-reduce(f32[2,256]{1,0:T(2,128)S(1)} %pad_maximum_fusion.4), channel_id=1, replica_groups=mesh['dp'=32] {'dp'}, use_global_device_ids=true, to_apply=%region_5.6 | all-reduce | flops 512 | bytes 4096 | tf_op jit(solution)/shard_map/psum | solution.py:58
  184.2 6.2 rev.7
  190.4 40.0 %all-reduce.7 = (f32[]{:T(128)}, f32[2,256]{1,0:T(2,128)}) all-reduce(f32[]{:T(128)} %fusion.100, f32[2,256]{1,0:T(2,128)S(1)} %pad_maximum_fusion.5), channel_id=1, replica_groups=mesh['dp'=32] {'dp'}, use_global_device_ids=true, to_apply=%region_17.18 | all-reduce | flops 513 | bytes 4104 | tf_op jit(solution)/shard_map/psum | solution.py:58
  250.3 40.8 %psum.89 = f32[2,256]{1,0:T(2,128)} all-reduce(f32[2,256]{1,0:T(2,128)} %pad_maximum_fusion.6), channel_id=1, replica_groups=mesh['dp'=32] {'dp'}, use_global_device_ids=true, to_apply=%region_21.22 | all-reduce | flops 512 | bytes 4096 | tf_op jit(solution)/shard_map/psum | solution.py:71
  296.2 9.5 %fusion.131 = f32[2304,256]{1,0:T(8,128)} fusion(bf16[2560,2304]{1,0:T(8,128)(2,1)} %copy-done.27, bf16[2560,256]{1,0:T(8,128)(2,1)S(1)} %fusion.60), kind=kOutput, calls=%fused_computation.343 | convolution fusion | flops 3019898880 | bytes 15466496 | tf_op jit(solution)/shard_map/dot_general | solution.py:48
  311.1 7.1 pad_slice_fusion.8
  322.1 7.0 fusion.110
  329.7 40.3 %psum.90 = f32[2,256]{1,0:T(2,128)} all-reduce(f32[2,256]{1,0:T(2,128)} %pad_maximum_fusion.7), channel_id=1, replica_groups=mesh['dp'=32] {'dp'}, use_global_device_ids=true, to_apply=%region_24.25 | all-reduce | flops 512 | bytes 4096 | tf_op jit(solution)/shard_map/psum | solution.py:71
  374.5 9.5 %fusion.130 = f32[2304,256]{1,0:T(8,128)} fusion(bf16[2560,2304]{1,0:T(8,128)(2,1)} %constant_dynamic-update-slice_fusion.1, bf16[2560,256]{1,0:T(8,128)(2,1)S(1)} %multiply_convert_fusion), kind=kOutput, calls=%fused_computation.342 | convolution fusion | flops 3019898880 | bytes 15466496 | tf_op jit(solution)/shard_map/dot_general | solution.py:48
  396.2 7.6 pad_slice_fusion
  420.5 11.1 %fusion.109 = (f32[256]{0:T(256)S(1)}, f32[256]{0:T(256)S(1)}, f32[2560,256]{1,0:T(8,128)}) fusion(f32[256]{0:T(256)S(1)} %bitcast.298, f32[2560,256]{1,0:T(8,128)S(1)} %get-tuple-element.194, f32[256]{0:T(256)S(1)} %bitcast.302, f32[256]{0:T(256)S(1)} %bitcast.314, f32[256]{0:T(256)S(1)} %bitcast.317, ...), kind=kOutput, calls=%fused_computation.328 | convolution fusion | flops 3036937728 | bytes 18225152 | tf_op jit(solution)/shard_map/dot_general | solution.py:102
  431.6 40.7 %psum.93 = f32[2,256]{1,0:T(2,128)S(1)} all-reduce(f32[2,256]{1,0:T(2,128)S(1)} %pad_maximum_fusion.8), channel_id=1, replica_groups=mesh['dp'=32] {'dp'}, use_global_device_ids=true, to_apply=%region_39.40 | all-reduce | flops 512 | bytes 4096 | tf_op jit(solution)/shard_map/psum | solution.py:71
  477.9 41.1 %all-reduce.6 = (f32[1]{0:T(128)}, f32[27,256]{1,0:T(8,128)S(1)}, f32[257,10]{0,1:T(8,128)S(1)}) all-reduce(f32[1]{0:T(128)} %bitcast.40, f32[27,256]{1,0:T(8,128)S(1)} %fusion.27, f32[257,10]{0,1:T(8,128)S(1)} %pad_maximum_fusion.2), channel_id=1, replica_groups=mesh['dp'=32] {'dp'}, use_global_device_ids=true, to_apply=%region_15.16 | all-reduce | flops 9483 | bytes 75864 | tf_op jit(solution)/shard_map/psum | solution.py:282
  522.9 43.0 %all-reduce.11.cloned.1.call-done = (f32[1024,256]{1,0:T(8,128)}, f32[18,256,256]{2,1,0:T(8,128)}) async-done(((f32[1024,256]{1,0:T(8,128)}, f32[18,256,256]{2,1,0:T(8,128)}), (f32[1024,256]{1,0:T(8,128)}, f32[18,256,256]{2,1,0:T(8,128)})) %all-reduce.11.cloned.1.call-update) | async-done | bytes 5767184 | tf_op jit(solution)/shard_map/psum | solution.py:258
  585.1 47.1 %custom-call.16 = f32[4,128,128]{2,1,0:T(8,128)S(1)} custom-call(f32[4,128,128]{2,1,0:T(8,128)S(1)} %cholesky.119), custom_call_target="Cholesky" | custom-call | tf_op jit(solution)/shard_map/jit(cholesky)/cholesky | solution.py:271
  633.3 39.3 %custom-call.17 = f32[4,1,128,128]{2,3,1,0:T(8,128)S(1)} custom-call(f32[4,1,128,128]{3,2,1,0:T(8,128)S(1)} %select_bitcast_fusion), custom_call_target="InvertDiagBlocksLowerTriangular" | custom-call | tf_op jit(solution)/shard_map/jit(cholesky)/cholesky | solution.py:271
  676.3 46.9 %custom-call.18 = f32[4,128,128]{2,1,0:T(8,128)S(1)} custom-call(f32[4,128,128]{2,1,0:T(8,128)S(1)} %convolution_subtract_fusion.1), custom_call_target="Cholesky" | custom-call | tf_op jit(solution)/shard_map/jit(cholesky)/cholesky | solution.py:271
  726.7 7.5 while.1
  734.2 79.8 %custom-call.19 = f32[4,2,128,128]{2,3,1,0:T(8,128)S(1)} custom-call(f32[4,2,128,128]{3,2,1,0:T(8,128)} %bitcast.353), custom_call_target="InvertDiagBlocksLowerTriangular" | custom-call | tf_op jit(solution)/shard_map/triangular_solve | solution.py:272
  839.2 6.7 reshape.350
  845.9 7.0 multiply_reduce_fusion
  (327 shorter events, 216.8 us)
Async XLA Ops:
  7.2 10.7 %copy-start.8 = (bf16[10,16,16,3]{2,1,3,0:T(8,128)(2,1)S(1)}, bf16[10,16,16,3]{2,1,3,0:T(8,128)(2,1)}, u32[]{:S(2)}) copy-start(bf16[10,16,16,3]{2,1,3,0:T(8,128)(2,1)} %param.16) | copy-start | bytes 46084
  7.2 87.8 %all-gather.3.cloned.1.call-start = ((), (), s32[]{:S(2)}) async-start(), calls=%async_computation | async-start | bytes 2433024 | tf_op jit(solution)/shard_map/all_gather | solution.py:169
  8.8 557.1 %all-reduce.11.cloned.1.call-start = ((), (), s32[]{:S(2)}) async-start(), calls=%async_computation.2 | async-start | bytes 11534336 | tf_op jit(solution)/shard_map/psum | solution.py:258
  65.3 22.4 %copy-start.40 = (f32[1,256]{1,0:T(1,128)}, f32[1,256]{1,0:T(1,128)S(1)}, u32[]{:S(2)}) copy-start(f32[1,256]{1,0:T(1,128)S(1)} %get-tuple-element.124) | copy-start | bytes 3076
  184.1 46.3 %copy-start.71 = (s32[10]{0:T(128)S(1)}, s32[10]{0:T(128)}, u32[]{:S(2)}) copy-start(s32[10]{0:T(128)} %param.18) | copy-start | bytes 124
  413.3 425.9 %all-gather.5.cloned.1.call-start = ((), (), s32[]{:S(2)}) async-start(), calls=%async_computation.1 | async-start | bytes 4866048 | tf_op jit(solution)/shard_map/all_gather | solution.py:296
  420.4 52.0 %copy-start.24 = (f32[10,256]{1,0:T(8,128)S(1)}, f32[10,256]{1,0:T(8,128)}, u32[]{:S(2)}) copy-start(f32[10,256]{1,0:T(8,128)} %reduce_sum.241) | copy-start | bytes 30724
  420.4 52.0 %copy-start.50 = (bf16[10,10]{0,1:T(8,128)(2,1)S(1)}, bf16[10,10]{0,1:T(8,128)(2,1)}, u32[]{:S(2)}) copy-start(bf16[10,10]{0,1:T(8,128)(2,1)} %copy-done.49) | copy-start | bytes 604
  420.4 52.1 %copy-start.35 = (f32[1,10]{0,1:T(8,128)S(1)}, f32[1,10]{0,1:T(8,128)}, u32[]{:S(2)}) copy-start(f32[1,10]{0,1:T(8,128)} %copy.79) | copy-start | bytes 124
  420.4 52.6 %copy-start.57 = (f32[1,256]{1,0:T(1,128)S(1)}, f32[1,256]{1,0:T(1,128)}, u32[]{:S(2)}) copy-start(f32[1,256]{1,0:T(1,128)} %get-tuple-element.129) | copy-start | bytes 3076
  420.5 52.6 %copy-start.63 = (f32[1,256]{1,0:T(1,128)S(1)}, f32[1,256]{1,0:T(1,128)}, u32[]{:S(2)}) copy-start(f32[1,256]{1,0:T(1,128)} %copy-done.62) | copy-start | bytes 3076
  420.5 52.6 %copy-start.65 = (f32[1,256]{1,0:T(1,128)S(1)}, f32[1,256]{1,0:T(1,128)}, u32[]{:S(2)}) copy-start(f32[1,256]{1,0:T(1,128)} %copy-done.64) | copy-start | bytes 3076
  420.5 52.6 %copy-start.70 = (f32[1,256]{1,0:T(1,128)S(1)}, f32[1,256]{1,0:T(1,128)}, u32[]{:S(2)}) copy-start(f32[1,256]{1,0:T(1,128)} %get-tuple-element.123) | copy-start | bytes 3076
  473.1 48.4 %copy-start.32 = (f32[257,10]{0,1:T(8,128)S(1)}, f32[257,10]{0,1:T(8,128)}, u32[]{:S(2)}) copy-start(f32[257,10]{0,1:T(8,128)} %param.26) | copy-start | bytes 30844
  473.1 48.4 %copy-start.37 = (f32[257,10]{0,1:T(8,128)S(1)}, f32[257,10]{0,1:T(8,128)}, u32[]{:S(2)}) copy-start(f32[257,10]{0,1:T(8,128)} %param.27) | copy-start | bytes 30844
  473.1 48.4 %copy-start.38 = (f32[257,10]{0,1:T(8,128)S(1)}, f32[257,10]{0,1:T(8,128)}, u32[]{:S(2)}) copy-start(f32[257,10]{0,1:T(8,128)} %param.28) | copy-start | bytes 30844
  473.1 49.0 %copy-start.29 = (f32[27,256]{1,0:T(8,128)S(1)}, f32[27,256]{1,0:T(8,128)}, u32[]{:S(2)}) copy-start(f32[27,256]{1,0:T(8,128)} %param.23) | copy-start | bytes 82948
  473.2 49.0 %copy-start.33 = (f32[27,256]{1,0:T(8,128)S(1)}, f32[27,256]{1,0:T(8,128)}, u32[]{:S(2)}) copy-start(f32[27,256]{1,0:T(8,128)} %param.24) | copy-start | bytes 82948
  473.2 49.0 %copy-start.34 = (f32[27,256]{1,0:T(8,128)S(1)}, f32[27,256]{1,0:T(8,128)}, u32[]{:S(2)}) copy-start(f32[27,256]{1,0:T(8,128)} %param.25) | copy-start | bytes 82948
  522.2 49.1 %copy-start.9 = (f32[4,256,256]{2,1,0:T(8,128)S(1)}, f32[4,256,256]{2,1,0:T(8,128)}, u32[]{:S(2)}) copy-start(f32[4,256,256]{2,1,0:T(8,128)} %param.22) | copy-start | bytes 3145732
  522.2 49.1 %copy-start.39 = (f32[144,2]{0,1:T(2,128)S(1)}, f32[144,2]{0,1:T(2,128)}, u32[]{:S(2)}) copy-start(f32[144,2]{0,1:T(2,128)} %compare_convert_fusion) | copy-start | bytes 3460
  582.4 50.9 %copy-start.31 = (pred[128,128]{1,0:T(8,128)(4,1)S(1)}, pred[128,128]{1,0:T(8,128)(4,1)}, u32[]{:S(2)}) copy-start(pred[128,128]{1,0:T(8,128)(4,1)} %iota_compare_fusion.2) | copy-start | bytes 49156
  585.1 138.1 %copy-start.30 = (pred[128,128]{1,0:T(8,128)(4,1)S(1)}, pred[128,128]{1,0:T(8,128)(4,1)}, u32[]{:S(2)}) copy-start(pred[128,128]{1,0:T(8,128)(4,1)} %iota_compare_fusion.3) | copy-start | bytes 49156
  633.3 93.3 %copy-start.72 = (s32[2]{0:T(128)S(1)}, s32[2]{0:T(128)}, u32[]{:S(2)}) copy-start(s32[2]{0:T(128)} %iota_multiply_fusion) | copy-start | bytes 28
  (52 other events, 207.2 us)
Sparse Core Ops, SparseCore 0:
  11.5 60.3 all-gather.2
  413.4 152.3 all-reduce.10
  572.7 63.2 all-gather.4
where the time goes:
time: 867 us; the launch traced here: 861 us
  blocking collectives  286 us (33%)
  other arithmetic  273 us (31%)
  local copies, waits for them, and re-layouts  135 us (16%)
  matrix products  108 us (12%)
  waiting for transfers between devices  43.1 us (5%)
  between operations  15.1 us (2%)
    another operation x10, other arithmetic, local(): lower_f = jnp.linalg.cholesky(gram_mat)  136 us
    psum x3, blocking collectives, pool_stats(): return lax.psum((moments(values), extra), 'dp')  123 us
    psum x3, blocking collectives, norm_back(): total_sums = lax.psum(local_sums, 'dp')  122 us
    another operation x5, other arithmetic, local(): lax.linalg.triangular_solve(lower_f, turned, left_side=False, lower=True,...  82.9 us
    psum x1, waiting for transfers between devices, local(): factor_all = lax.psum(factor_stack, 'dp')  43 us
    psum x1, blocking collectives, local(): lax.psum((conv_grad, stem_grad, head_grad, loss_local), 'dp')  41.1 us
    unnamed x185, local copies, waits for them, and re-layouts  35.3 us
    dot_general x8, matrix products, inner_rows(): lax.dot_general(left_in, right_in, (((0,), (0,)), ((), ())), preferred_el...  30 us
  transfers between devices with their start and end apart: 3, of which 1 were waited for; matrix products, arithmetic and copies ran while one was open for 39% of the time, Pallas kernels for 0%

commit v1 on v0

--- a/solution.py
+++ b/solution.py
@@ -50,12 +50,69 @@
     )
 
 
+def bit_groups(devices):
+    total_bits = devices.bit_length() - 1
+    groups = [(0, 1)]
+    while groups[-1][0] + groups[-1][1] < total_bits:
+        first = groups[-1][0] + groups[-1][1]
+        groups.append((first, min(2, total_bits - first)))
+    return groups
+
+
+def swap(values, mask, devices):
+    return lax.ppermute(values, "dp", [(i, i ^ mask) for i in range(devices)])
+
+
+def sum_small(values):
+    devices = lax.axis_size("dp")
+    copies = jnp.broadcast_to(values[None], (devices,) + values.shape)
+    return jnp.sum(lax.all_to_all(copies, "dp", 0, 0, tiled=True), axis=0)
+
+
+def gather_all(piece):
+    devices = lax.axis_size("dp")
+    me = lax.axis_index("dp")
+    groups = bit_groups(devices)[::-1]
+    held = piece[(None,) * len(groups)]
+    for axis, (first, width) in enumerate(groups):
+        radix = 1 << width
+        mine = (me >> first) & (radix - 1)
+        got = [held] + [swap(held, k << first, devices) for k in range(1, radix)]
+        ordered = []
+        for j in range(radix):
+            value = got[j]
+            for m in range(1, radix):
+                value = jnp.where(mine == m, got[j ^ m], value)
+            ordered.append(value)
+        held = jnp.concatenate(ordered, axis=axis)
+    return held.reshape((devices,) + piece.shape)
+
+
+def scatter_sum(pieces, sent_as):
+    devices = lax.axis_size("dp")
+    me = lax.axis_index("dp")
+    groups = bit_groups(devices)
+    held = pieces.reshape(tuple(1 << width for _, width in groups[::-1]) + pieces.shape[1:])
+    for order, (first, width) in enumerate(groups):
+        axis = len(groups) - 1 - order
+        radix = 1 << width
+        mine = (me >> first) & (radix - 1)
+        parts = [lax.dynamic_slice_in_dim(held, mine ^ k, 1, axis=axis) for k in range(radix)]
+        total = parts[0].astype(jnp.float32)
+        for k in range(1, radix):
+            total = total + swap(parts[k].astype(sent_as), k << first, devices).astype(jnp.float32)
+        held = total
+    return held.reshape(pieces.shape[1:])
+
+
 def moments(values):
     return jnp.stack([jnp.sum(values, axis=0), jnp.sum(values * values, axis=0)])
 
 
 def pool_stats(values, extra):
-    return lax.psum((moments(values), extra), "dp")
+    extra_row = jnp.full((1, values.shape[1]), extra, jnp.float32)
+    total = sum_small(jnp.concatenate([moments(values), extra_row], axis=0))
+    return total[:2], total[2, 0]
 
 
 def normalize(values, stat_sums, gain_row, shift_row, pixels):
@@ -68,7 +125,7 @@
 
 def norm_back(grad_out, centered, inv_std, gain_row, pixels):
     local_sums = jnp.stack([jnp.sum(grad_out, axis=0), jnp.sum(grad_out * centered, axis=0)])
-    total_sums = lax.psum(local_sums, "dp")
+    total_sums = sum_small(local_sums)
     grad_in = (
         inv_std
         * gain_row
@@ -120,21 +177,6 @@
         / (jnp.sqrt(second_new / (1.0 - BETA_TWO**STEP)) + ADAM_EPS)
     )
     return (param_in - rate_in * (direction + decay_in * param_in), first_new, second_new)
-
-
-def select_rows(stacked, pick_mask):
-    return jnp.sum(stacked * pick_mask[:, :, None], axis=1)
-
-
-def rotate_rows(selector, stacked, block_ids, layer_ids, right_q, pattern):
-    mixed_rows = jnp.einsum("rk,bkn->rbn", selector, stacked, precision=highest)
-    pick_block = (
-        block_ids[:, None] == jnp.arange(stacked.shape[0], dtype=jnp.int32)[None, :]
-    ).astype(jnp.float32)
-    left_rows = select_rows(mixed_rows, pick_block)
-    both_sides = jnp.einsum(pattern, left_rows, right_q, precision=highest)
-    pick_layer = (layer_ids[:, None] == jnp.arange(2, dtype=jnp.int32)[None, :]).astype(jnp.float32)
-    return select_rows(both_sides, pick_layer)
 
 
 def damp_all(factor_full, channels):
@@ -166,7 +208,7 @@
     count_img, side_len = (images.shape[0], images.shape[1])
     channels = conv_w.shape[1]
     pixels = count_img * side_len * side_len * devices
-    conv_gathered = lax.all_gather(conv_w.astype(jnp.bfloat16), "dp", axis=0, tiled=True)
+    conv_gathered = gather_all(conv_w.astype(jnp.bfloat16)).reshape(18 * channels, channels)
     conv_full = to_blocks(conv_gathered, 18).reshape(18 * channels, channels)
     weights_img = 1.0 + 3.0 * groups.astype(jnp.float32)
     stem_cols = patches(images)
@@ -251,18 +293,19 @@
             norm_sums[2][0],
         ]
     )
-    conv_grad = from_blocks(jnp.concatenate(conv_grads, axis=0).reshape(18, channels, channels))
     factor_stack = from_blocks(jnp.stack(factor_list))
     factor_count = factor_stack.shape[0] // devices
     identity = jnp.eye(channels, dtype=jnp.float32)
-    factor_all = lax.psum(factor_stack, "dp")
+    row_factor = scatter_sum(
+        factor_stack.reshape(devices, factor_count, channels), jnp.float32
+    )
+    factor_all = gather_all(row_factor).reshape(4 * channels, channels)
     factor_full = to_blocks(factor_all, 4)
     damped = damp_all(factor_full, channels)
     inverse = identity / jnp.sqrt(jnp.sum(damped * damped, axis=(1, 2)))[:, None, None]
     for sweep_id in range(NS_ITERS):
         product = jnp.einsum("mab,mbc->mac", inverse, damped, precision=highest)
         inverse = 2.0 * inverse - jnp.einsum("mab,mbc->mac", product, inverse, precision=highest)
-    row_factor = lax.dynamic_slice_in_dim(factor_all, my_index * factor_count, factor_count, 0)
     inverse_rows = lax.dynamic_slice_in_dim(
         from_blocks(inverse), my_index * factor_count, factor_count, 0
     )
@@ -274,18 +317,33 @@
     )
     left_q = rot_bases[0::2]
     right_q = rot_bases[1::2]
-    row_count = conv_w.shape[0]
-    global_row = my_index * row_count + jnp.arange(row_count, dtype=jnp.int32)
-    block_ids = global_row % 18
-    inner_ids = global_row // 18
-    layer_ids = block_ids // 9
-    conv_total, stem_total, head_total, loss_total = lax.psum(
-        (conv_grad, stem_grad, head_grad, loss_local), "dp"
-    )
-    selector = left_q.transpose(0, 2, 1)[layer_ids, inner_ids]
-    rotated = rotate_rows(
-        selector, to_blocks(conv_total, 18), block_ids, layer_ids, right_q, "rn,lnd->rld"
-    )
+    row_channels = channels // devices
+    tail_sums = jnp.concatenate(
+        [
+            stem_grad,
+            jnp.pad(head_grad.T, ((0, 0), (0, 2 * channels - head_grad.shape[0]))).reshape(-1, channels),
+            jnp.full((1, channels), loss_local, jnp.float32),
+        ],
+        axis=0,
+    )
+    tail_total = sum_small(tail_sums)
+    stem_rows = stem_w.shape[0]
+    stem_total = tail_total[:stem_rows]
+    head_total = tail_total[stem_rows : stem_rows + 2 * CLASSES].reshape(CLASSES, 2 * channels).T[: channels + 1]
+    loss_total = tail_total[-1, 0]
+    right_rot = []
+    for layer_id in range(2):
+        left_turned = jnp.einsum(
+            "ki,tkn->itn",
+            left_q[layer_id],
+            conv_grads[layer_id].reshape(9, channels, channels),
+            precision=lax.Precision.HIGH,
+        )
+        own_rows = scatter_sum(
+            left_turned.astype(jnp.bfloat16).reshape(devices, row_channels, 9, channels), jnp.bfloat16
+        )
+        right_rot.append(jnp.einsum("rtn,nd->rtd", own_rows, right_q[layer_id], precision=highest))
+    rotated = jnp.stack(right_rot, axis=1).reshape(-1, channels)
     first_conv = BETA_ONE * conv_m + (1.0 - BETA_ONE) * rotated
     second_conv = BETA_TWO * conv_v + (1.0 - BETA_TWO) * rotated * rotated
     direction = (
@@ -293,10 +351,20 @@
         / (1.0 - BETA_ONE**STEP)
         / (jnp.sqrt(second_conv / (1.0 - BETA_TWO**STEP)) + ADAM_EPS)
     )
-    steps_full = to_blocks(lax.all_gather(direction, "dp", axis=0, tiled=True), 18)
-    update = rotate_rows(
-        left_q[layer_ids, inner_ids], steps_full, block_ids, layer_ids, right_q, "rn,ldn->rld"
-    )
+    direction_own = direction.reshape(row_channels, 2, 9, channels)
+    updates = []
+    for layer_id in range(2):
+        half = jnp.einsum(
+            "rtn,dn->rtd", direction_own[:, layer_id], right_q[layer_id], precision=highest
+        )
+        full = gather_all(half.astype(jnp.bfloat16)).reshape(channels, 9 * channels)
+        own_left = lax.dynamic_slice_in_dim(left_q[layer_id], my_index * row_channels, row_channels, 0)
+        updates.append(
+            jnp.dot(own_left.astype(jnp.bfloat16), full, preferred_element_type=jnp.float32).reshape(
+                row_channels, 9, channels
+            )
+        )
+    update = jnp.stack(updates, axis=1).reshape(-1, channels)
     conv_new = conv_w - RATE_CONV * (update + WEIGHT_DECAY * conv_w)
     stem_new, stem_first, stem_second = adam_step(
         stem_w, stem_total, stem_m, stem_v, RATE_STEM, WEIGHT_DECAY

time: 867 us -> 722 us (0.83)
  blocking collectives: 286 us -> 0 us
  starting transfers between devices: 0.59 us -> 111 us
  local copies, waits for them, and re-layouts: 135 us -> 170 us
  other arithmetic: 273 us -> 288 us
  matrix products: 108 us -> 94.1 us
  between operations: 15.1 us -> 3.27 us
    psum x7 -> x0, blocking collectives: 286 us -> none  [the longest x3 123 us: pool_stats(): return lax.psum((moments(values), extra), 'dp')]
    ppermute x0 -> x49, starting transfers between devices: none -> 63 us  [swap(): return lax.ppermute(values, 'dp', [(i, i ^ mask) for i in range(devices)])]
    all_to_all x0 -> x7, starting transfers between devices: none -> 47.9 us  [sum_small(): return jnp.sum(lax.all_to_all(copies, 'dp', 0, 0, tiled=True), axis=0)]
    psum x1 -> x0, waiting for transfers between devices: 43 us -> none  [local(): factor_all = lax.psum(factor_stack, 'dp')]
    ppermute x0 -> x49, waiting for transfers between devices: none -> 39 us  [swap(): return lax.ppermute(values, 'dp', [(i, i ^ mask) for i in range(devices)])]
    dot_general x0 -> x4, local copies, waits for them, and re-layouts: none -> 34.7 us  [the longest x2 30.8 us: inner_rows(): lax.dot_general(left_in, right_in, (((0,), (0,)), ((), ())), preferred_el...]
    reshape x3 -> x5, local copies, waits for them, and re-layouts: 12.5 us -> 0.1 us  [the longest x1 0.03 us: local(): rotated = jnp.stack(right_rot, axis=1).reshape(-1, channels)]
    unnamed x185 -> x263, local copies, waits for them, and re-layouts: 35.3 us -> 42.3 us
  transfers between devices with their start and end apart: 3 -> 56, of which waited for: 1 -> 17; matrix products, arithmetic and copies ran while one was open for 39% -> 65% of each run, Pallas kernels for 0% -> 0%
where the time goes in v1:
time: 722 us; the launch traced here: 710 us
  other arithmetic  288 us (40%)
  local copies, waits for them, and re-layouts  170 us (24%)
  starting transfers between devices  111 us (15%)
  matrix products  94.1 us (13%)
  waiting for transfers between devices  44.3 us (6%)
    another operation x9, other arithmetic, local(): lower_f = jnp.linalg.cholesky(gram_mat)  141 us
    another operation x5, other arithmetic, local(): lax.linalg.triangular_solve(lower_f, turned, left_side=False, lower=True,...  84.7 us
    ppermute x49, starting transfers between devices, swap(): return lax.ppermute(values, 'dp', [(i, i ^ mask) for i in range(devices)])  63 us
    all_to_all x7, starting transfers between devices, sum_small(): return jnp.sum(lax.all_to_all(copies, 'dp', 0, 0, tiled=True), axis=0)  47.9 us
    unnamed x263, local copies, waits for them, and re-layouts  42.3 us
    ppermute x49, waiting for transfers between devices, swap(): return lax.ppermute(values, 'dp', [(i, i ^ mask) for i in range(devices)])  39 us
    dot_general x2, local copies, waits for them, and re-layouts, inner_rows(): lax.dot_general(left_in, right_in, (((0,), (0,)), ((), ())), preferred_el...  30.8 us
    dot_general x8, matrix products, inner_rows(): lax.dot_general(left_in, right_in, (((0,), (0,)), ((), ())), preferred_el...  25 us
  transfers between devices with their start and end apart: 56, of which 17 were waited for; matrix products, arithmetic and copies ran while one was open for 65% of the time, Pallas kernels for 0%

profile of v1, /device:TPU:0, one launch (start us, length us, event | category | flops | bytes accessed | tf_op | source)
XLA Modules:
  0.0 710.2 jit_solution(2631882935766395893)
XLA Ops:
  22.4 6.2 all-to-all-start
  69.1 15.4 %copy.181 = bf16[2304,2560]{1,0:T(8,128)(2,1)} copy(bf16[2304,2560]{0,1:T(8,128)(2,1)} %bitcast.99) | data formatting | bytes 23592960 | tf_op jit(solution)/shard_map/dot_general | solution.py:48
  90.8 5.2 reshape_reshape_reshape.9
  101.0 9.5 %fusion.110 = (f32[256]{0:T(256)S(1)}, f32[256]{0:T(256)S(1)}, f32[2560,256]{1,0:T(8,128)}) fusion(bf16[2560,2304]{1,0:T(8,128)(2,1)} %constant_dynamic-update-slice_fusion.1, bf16[2304,256]{1,0:T(8,128)(2,1)S(1)} %bitcast.375), kind=kOutput, calls=%fused_computation.415 | convolution fusion | flops 3021864448 | bytes 15599616 | tf_op jit(solution)/shard_map/dot_general | solution.py:145
  111.3 6.0 all-to-all-start.1
  121.5 6.3 rev.6
  127.8 6.3 rev.7
  159.8 15.2 %all-to-all-start.2 = ((f32[32,3,256]{2,1,0:T(4,128)}), f32[32,3,256]{2,1,0:T(4,128)S(1)}, u32[]{:S(2)}, u32[]{:S(2)}) async-start(f32[32,3,256]{2,1,0:T(4,128)} %broadcast_in_dim.41), calls=%async_computation.2 | async-start | bytes 262144 | tf_op jit(solution)/shard_map/all_to_all | solution.py:69
  175.0 15.3 %copy.185 = bf16[2304,2560]{1,0:T(8,128)(2,1)} copy(bf16[2304,2560]{0,1:T(8,128)(2,1)} %bitcast.326) | data formatting | bytes 23592960 | tf_op jit(solution)/shard_map/dot_general | solution.py:48
  205.9 5.7 all-to-all-start.3
  213.6 5.4 all-to-all-done.3
  229.9 7.1 fusion.107
  240.4 6.6 fusion.22
  262.0 7.5 %pad_slice_fusion = (bf16[10,16,16,256]{3,2,1,0:T(8,128)(2,1)S(1)}, bf16[10,16,16,256]{3,2,1,0:T(8,128)(2,1)S(1)}, bf16[10,16,16,256]{3,2,1,0:T(8,128)(2,1)S(1)}...) fusion(bf16[10,16,16,256]{3,2,1,0:T(8,128)(2,1)} %bitcast.321), kind=kLoop, calls=%fused_computation.11 | loop fusion | bytes 11796480 | tf_op jit(solution)/shard_map/slice | solution.py:40
  272.5 7.0 fusion.106
  280.2 5.9 all-to-all-start.5
  286.2 6.6 fusion.24
  302.2 6.0 all-to-all-start.6
  319.9 5.3 collective-permute-done.29
  423.6 48.1 %custom-call.16 = f32[4,128,128]{2,1,0:T(8,128)S(1)} custom-call(f32[4,128,128]{2,1,0:T(8,128)} %cholesky.119), custom_call_target="Cholesky" | custom-call | tf_op jit(solution)/shard_map/jit(cholesky)/cholesky | solution.py:314
  473.4 40.7 %custom-call.17 = f32[4,1,128,128]{2,3,1,0:T(8,128)} custom-call(f32[4,1,128,128]{3,2,1,0:T(8,128)} %select_bitcast_fusion), custom_call_target="InvertDiagBlocksLowerTriangular" | custom-call | tf_op jit(solution)/shard_map/jit(cholesky)/cholesky | solution.py:314
  518.6 48.3 %custom-call.18 = f32[4,128,128]{2,1,0:T(8,128)} custom-call(f32[4,128,128]{2,1,0:T(8,128)} %convolution_subtract_fusion.1), custom_call_target="Cholesky" | custom-call | tf_op jit(solution)/shard_map/jit(cholesky)/cholesky | solution.py:314
  571.3 7.5 %while.1 = (s32[]{:T(128)}, f32[4,256,256]{2,1,0:T(8,128)}, s32[2,2]{1,0:T(2,128)S(1)}, f32[2,4,128,128]{3,2,0,1:T(8,128)}, s32[]{:T(128)}) while((s32[]{:T(128)}, f32[4,256,256]{2,1,0:T(8,128)}, s32[2,2]{1,0:T(2,128)S(1)}, f32[2,4,128,128]{3,2,0,1:T(8,128)}, s32[]{:T(128)}) %tuple.151), condition=%wide.while_cond, body=%wide.while_body.sunk | while | flops 2 | bytes 525421 | solution.py:315
  578.8 80.2 %custom-call.19 = f32[4,2,128,128]{2,3,1,0:T(8,128)} custom-call(f32[4,2,128,128]{3,2,1,0:T(8,128)} %bitcast.443), custom_call_target="InvertDiagBlocksLowerTriangular" | custom-call | tf_op jit(solution)/shard_map/triangular_solve | solution.py:315
  (579 shorter events, 341.1 us)
Async XLA Ops:
  2.2 37.7 %collective-permute-start.2 = (bf16[1,1,1,144,256]{4,3,2,1,0:T(8,128)(2,1)}, bf16[1,1,1,144,256]{4,3,2,1,0:T(8,128)(2,1)}, u32[]{:S(2)}, u32[]{:S(2)}) collective-permute-start(bf16[1,1,1,144,256]{4,3,2,1,0:T(8,128)(2,1)} %convert_bitcast_fusion), channel_id=1, source_target_pairs={{0,8},{1,9},{2,10},{3,11},{4,12},{5,13},{6,14},{7,15},{8,0},{9,1},... | collective-permute-start | bytes 221192 | tf_op jit(solution)/shard_map/ppermute | solution.py:63
  5.2 34.7 %collective-permute-start.1 = (bf16[1,1,1,144,256]{4,3,2,1,0:T(8,128)(2,1)}, bf16[1,1,1,144,256]{4,3,2,1,0:T(8,128)(2,1)}, u32[]{:S(2)}, u32[]{:S(2)}) collective-permute-start(bf16[1,1,1,144,256]{4,3,2,1,0:T(8,128)(2,1)} %convert_bitcast_fusion), channel_id=1, source_target_pairs={{0,16},{1,17},{2,18},{3,19},{4,20},{5,21},{6,22},{7,23},{8,24},{9,... | collective-permute-start | bytes 221192 | tf_op jit(solution)/shard_map/ppermute | solution.py:63
  7.8 32.1 %collective-permute-start = (bf16[1,1,1,144,256]{4,3,2,1,0:T(8,128)(2,1)}, bf16[1,1,1,144,256]{4,3,2,1,0:T(8,128)(2,1)}, u32[]{:S(2)}, u32[]{:S(2)}) collective-permute-start(bf16[1,1,1,144,256]{4,3,2,1,0:T(8,128)(2,1)} %convert_bitcast_fusion), channel_id=1, source_target_pairs={{0,24},{1,25},{2,26},{3,27},{4,28},{5,29},{6,30},{7,31},{8,16},{9,... | collective-permute-start | bytes 221192 | tf_op jit(solution)/shard_map/ppermute | solution.py:63
  22.4 23.4 %all-to-all-start = ((f32[32,3,256]{2,1,0:T(4,128)}), f32[32,3,256]{2,1,0:T(4,128)}, u32[]{:S(2)}, u32[]{:S(2)}) async-start(f32[32,3,256]{2,1,0:T(4,128)} %broadcast_in_dim.38), calls=%async_computation | async-start | bytes 262144 | tf_op jit(solution)/shard_map/all_to_all | solution.py:69
  42.3 18.7 %collective-permute-start.5 = (bf16[4,1,1,144,256]{4,3,2,1,0:T(8,128)(2,1)}, bf16[4,1,1,144,256]{4,3,2,1,0:T(8,128)(2,1)}, u32[]{:S(2)}, u32[]{:S(2)}) collective-permute-start(bf16[4,1,1,144,256]{4,3,2,1,0:T(8,128)(2,1)} %pad_maximum_fusion.9), channel_id=1, source_target_pairs={{0,2},{1,3},{2,0},{3,1},{4,6},{5,7},{6,4},{7,5},{8,10},{9,11},{10,... | collective-permute-start | bytes 884744 | tf_op jit(solution)/shard_map/ppermute | solution.py:63
  44.0 17.0 %collective-permute-start.4 = (bf16[4,1,1,144,256]{4,3,2,1,0:T(8,128)(2,1)}, bf16[4,1,1,144,256]{4,3,2,1,0:T(8,128)(2,1)}, u32[]{:S(2)}, u32[]{:S(2)}) collective-permute-start(bf16[4,1,1,144,256]{4,3,2,1,0:T(8,128)(2,1)} %pad_maximum_fusion.9), channel_id=1, source_target_pairs={{0,4},{1,5},{2,6},{3,7},{4,0},{5,1},{6,2},{7,3},{8,12},{9,13},{10,... | collective-permute-start | bytes 884744 | tf_op jit(solution)/shard_map/ppermute | solution.py:63
  64.7 22.9 %collective-permute-start.6 = (bf16[4,4,1,144,256]{4,3,2,1,0:T(8,128)(2,1)}, bf16[4,4,1,144,256]{4,3,2,1,0:T(8,128)(2,1)}, u32[]{:S(2)}, u32[]{:S(2)}) collective-permute-start(bf16[4,4,1,144,256]{4,3,2,1,0:T(8,128)(2,1)} %pad_maximum_fusion.3), channel_id=1, source_target_pairs={{0,1},{1,0},{2,3},{3,2},{4,5},{5,4},{6,7},{7,6},{8,9},{9,8},{10,11... | collective-permute-start | bytes 3538952 | tf_op jit(solution)/shard_map/ppermute | solution.py:63
  111.3 31.1 %all-to-all-start.1 = ((f32[32,3,256]{2,1,0:T(4,128)}), f32[32,3,256]{2,1,0:T(4,128)S(1)}, u32[]{:S(2)}, u32[]{:S(2)}) async-start(f32[32,3,256]{2,1,0:T(4,128)} %broadcast_in_dim.40), calls=%async_computation.1 | async-start | bytes 262144 | tf_op jit(solution)/shard_map/all_to_all | solution.py:69
  159.8 32.9 %all-to-all-start.2 = ((f32[32,3,256]{2,1,0:T(4,128)}), f32[32,3,256]{2,1,0:T(4,128)S(1)}, u32[]{:S(2)}, u32[]{:S(2)}) async-start(f32[32,3,256]{2,1,0:T(4,128)} %broadcast_in_dim.41), calls=%async_computation.2 | async-start | bytes 262144 | tf_op jit(solution)/shard_map/all_to_all | solution.py:69
  250.0 59.0 %collective-permute-start.28 = (bf16[4,4,1,8,9,256]{5,3,4,2,1,0:T(8,128)(2,1)}, bf16[4,4,1,8,9,256]{5,3,4,2,1,0:T(8,128)(2,1)}, u32[]{:S(2)}, u32[]{:S(2)}) collective-permute-start(bf16[4,4,1,8,9,256]{5,3,4,2,1,0:T(8,128)(2,1)} %copy.248), channel_id=1, source_target_pairs={{0,1},{1,0},{2,3},{3,2},{4,5},{5,4},{6,7},{7,6},{8,9},{9,8},{10,11... | collective-permute-start | bytes 1769480 | tf_op jit(solution)/shard_map/ppermute | solution.py:63
  261.7 52.4 %collective-permute-start.7 = (f32[4,4,1,32,256]{4,3,2,1,0:T(8,128)}, f32[4,4,1,32,256]{4,3,2,1,0:T(8,128)}, u32[]{:S(2)}, u32[]{:S(2)}) collective-permute-start(f32[4,4,1,32,256]{4,3,2,1,0:T(8,128)} %constant_dynamic-slice_fusion.14), channel_id=1, source_target_pairs={{0,1},{1,0},{2,3},{3,2},{4,5},{5,4},{6,7},{7,6},{8,9},{9,8},{10,11... | collective-permute-start | bytes 1572872 | tf_op jit(solution)/shard_map/ppermute | solution.py:63
  295.8 21.4 %collective-permute-start.21 = (bf16[4,4,1,8,9,256]{5,3,4,2,1,0:T(8,128)(2,1)}, bf16[4,4,1,8,9,256]{5,3,4,2,1,0:T(8,128)(2,1)}, u32[]{:S(2)}, u32[]{:S(2)}) collective-permute-start(bf16[4,4,1,8,9,256]{5,3,4,2,1,0:T(8,128)(2,1)} %copy.245), channel_id=1, source_target_pairs={{0,1},{1,0},{2,3},{3,2},{4,5},{5,4},{6,7},{7,6},{8,9},{9,8},{10,11... | collective-permute-start | bytes 1769480 | tf_op jit(solution)/shard_map/ppermute | solution.py:63
  302.2 402.3 %all-to-all-start.6 = ((f32[32,48,256]{2,1,0:T(8,128)}), f32[32,48,256]{2,1,0:T(8,128)}, u32[]{:S(2)}, u32[]{:S(2)}) async-start(f32[32,48,256]{2,1,0:T(8,128)} %broadcast_in_dim.48), calls=%async_computation.6 | async-start | bytes 3145728 | tf_op jit(solution)/shard_map/all_to_all | solution.py:69
  312.4 21.0 %collective-permute-start.31 = (bf16[4,1,1,8,9,256]{5,3,4,2,1,0:T(8,128)(2,1)S(1)}, bf16[4,1,1,8,9,256]{5,3,4,2,1,0:T(8,128)(2,1)S(1)}, u32[]{:S(2)}, u32[]{:S(2)}) collective-permute-start(bf16[4,1,1,8,9,256]{5,3,4,2,1,0:T(8,128)(2,1)S(1)} %get-tuple-element.207), channel_id=1, source_target_pairs={{0,6},{1,7},{2,4},{3,5},{4,2},{5,3},{6,0},{7,1},{8,14},{9,15},{10,... | collective-permute-start | bytes 442376 | tf_op jit(solution)/shard_map/ppermute | solution.py:63
  313.9 20.5 %collective-permute-start.30 = (bf16[4,1,1,8,9,256]{5,3,4,2,1,0:T(8,128)(2,1)S(1)}, bf16[4,1,1,8,9,256]{5,3,4,2,1,0:T(8,128)(2,1)S(1)}, u32[]{:S(2)}, u32[]{:S(2)}) collective-permute-start(bf16[4,1,1,8,9,256]{5,3,4,2,1,0:T(8,128)(2,1)S(1)} %get-tuple-element.208), channel_id=1, source_target_pairs={{0,4},{1,5},{2,6},{3,7},{4,0},{5,1},{6,2},{7,3},{8,12},{9,13},{10,... | collective-permute-start | bytes 442376 | tf_op jit(solution)/shard_map/ppermute | solution.py:63
  315.2 20.6 %collective-permute-start.8 = (f32[4,1,1,32,256]{4,3,2,1,0:T(8,128)S(1)}, f32[4,1,1,32,256]{4,3,2,1,0:T(8,128)S(1)}, u32[]{:S(2)}, u32[]{:S(2)}) collective-permute-start(f32[4,1,1,32,256]{4,3,2,1,0:T(8,128)S(1)} %get-tuple-element.229), channel_id=1, source_target_pairs={{0,2},{1,3},{2,0},{3,1},{4,6},{5,7},{6,4},{7,5},{8,10},{9,11},{10,... | collective-permute-start | bytes 393224 | tf_op jit(solution)/shard_map/ppermute | solution.py:63
  317.2 22.5 %collective-permute-start.10 = (f32[4,1,1,32,256]{4,3,2,1,0:T(8,128)S(1)}, f32[4,1,1,32,256]{4,3,2,1,0:T(8,128)S(1)}, u32[]{:S(2)}, u32[]{:S(2)}) collective-permute-start(f32[4,1,1,32,256]{4,3,2,1,0:T(8,128)S(1)} %get-tuple-element.230), channel_id=1, source_target_pairs={{0,6},{1,7},{2,4},{3,5},{4,2},{5,3},{6,0},{7,1},{8,14},{9,15},{10,... | collective-permute-start | bytes 393224 | tf_op jit(solution)/shard_map/ppermute | solution.py:63
  325.2 16.8 %collective-permute-start.9 = (f32[4,1,1,32,256]{4,3,2,1,0:T(8,128)S(1)}, f32[4,1,1,32,256]{4,3,2,1,0:T(8,128)S(1)}, u32[]{:S(2)}, u32[]{:S(2)}) collective-permute-start(f32[4,1,1,32,256]{4,3,2,1,0:T(8,128)S(1)} %get-tuple-element.231), channel_id=1, source_target_pairs={{0,4},{1,5},{2,6},{3,7},{4,0},{5,1},{6,2},{7,3},{8,12},{9,13},{10,... | collective-permute-start | bytes 393224 | tf_op jit(solution)/shard_map/ppermute | solution.py:63
  333.4 28.4 %collective-permute-start.22 = (bf16[4,1,1,8,9,256]{5,3,4,2,1,0:T(8,128)(2,1)S(1)}, bf16[4,1,1,8,9,256]{5,3,4,2,1,0:T(8,128)(2,1)S(1)}, u32[]{:S(2)}, u32[]{:S(2)}) collective-permute-start(bf16[4,1,1,8,9,256]{5,3,4,2,1,0:T(8,128)(2,1)S(1)} %get-tuple-element.201), channel_id=1, source_target_pairs={{0,2},{1,3},{2,0},{3,1},{4,6},{5,7},{6,4},{7,5},{8,10},{9,11},{10,... | collective-permute-start | bytes 442376 | tf_op jit(solution)/shard_map/ppermute | solution.py:63
  334.4 27.5 %collective-permute-start.24 = (bf16[4,1,1,8,9,256]{5,3,4,2,1,0:T(8,128)(2,1)S(1)}, bf16[4,1,1,8,9,256]{5,3,4,2,1,0:T(8,128)(2,1)S(1)}, u32[]{:S(2)}, u32[]{:S(2)}) collective-permute-start(bf16[4,1,1,8,9,256]{5,3,4,2,1,0:T(8,128)(2,1)S(1)} %get-tuple-element.202), channel_id=1, source_target_pairs={{0,6},{1,7},{2,4},{3,5},{4,2},{5,3},{6,0},{7,1},{8,14},{9,15},{10,... | collective-permute-start | bytes 442376 | tf_op jit(solution)/shard_map/ppermute | solution.py:63
  368.0 21.1 %collective-permute-start.19 = (f32[4,1,1,32,256]{4,3,2,1,0:T(8,128)S(1)}, f32[4,1,1,32,256]{4,3,2,1,0:T(8,128)S(1)}, u32[]{:S(2)}, u32[]{:S(2)}) collective-permute-start(f32[4,1,1,32,256]{4,3,2,1,0:T(8,128)S(1)} %pad_maximum_fusion.14), channel_id=1, source_target_pairs={{0,2},{1,3},{2,0},{3,1},{4,6},{5,7},{6,4},{7,5},{8,10},{9,11},{10,... | collective-permute-start | bytes 393224 | tf_op jit(solution)/shard_map/ppermute | solution.py:63
  369.4 21.8 %collective-permute-start.18 = (f32[4,1,1,32,256]{4,3,2,1,0:T(8,128)S(1)}, f32[4,1,1,32,256]{4,3,2,1,0:T(8,128)S(1)}, u32[]{:S(2)}, u32[]{:S(2)}) collective-permute-start(f32[4,1,1,32,256]{4,3,2,1,0:T(8,128)S(1)} %pad_maximum_fusion.14), channel_id=1, source_target_pairs={{0,4},{1,5},{2,6},{3,7},{4,0},{5,1},{6,2},{7,3},{8,12},{9,13},{10,... | collective-permute-start | bytes 393224 | tf_op jit(solution)/shard_map/ppermute | solution.py:63
  409.2 281.7 %collective-permute-start.48 = (bf16[4,4,1,8,9,256]{5,3,4,2,1,0:T(8,128)(2,1)}, bf16[4,4,1,8,9,256]{5,3,4,2,1,0:T(8,128)(2,1)}, u32[]{:S(2)}, u32[]{:S(2)}) collective-permute-start(bf16[4,4,1,8,9,256]{5,3,4,2,1,0:T(8,128)(2,1)} %copy.197), channel_id=1, source_target_pairs={{0,1},{1,0},{2,3},{3,2},{4,5},{5,4},{6,7},{7,6},{8,9},{9,8},{10,11... | collective-permute-start | bytes 1769480 | tf_op jit(solution)/shard_map/ppermute | solution.py:63
  410.7 285.9 %collective-permute-start.41 = (bf16[4,4,1,8,9,256]{5,3,4,2,1,0:T(8,128)(2,1)}, bf16[4,4,1,8,9,256]{5,3,4,2,1,0:T(8,128)(2,1)}, u32[]{:S(2)}, u32[]{:S(2)}) collective-permute-start(bf16[4,4,1,8,9,256]{5,3,4,2,1,0:T(8,128)(2,1)} %copy.191), channel_id=1, source_target_pairs={{0,1},{1,0},{2,3},{3,2},{4,5},{5,4},{6,7},{7,6},{8,9},{9,8},{10,11... | collective-permute-start | bytes 1769480 | tf_op jit(solution)/shard_map/ppermute | solution.py:63
  (141 other events, 1262.0 us)
